TPU v7x, 128 devices: a whole 4x4x4 slice. The times are simulated.
128 devices in a mesh: member: 32 (over z_lo, y, x), space: 4 (over z_hi, core).
Axes of the slice: x: 4, y: 4, z: 4 (z_hi: 2, z_lo: 2; z = z_hi * 2 + z_lo), core: 2. Of those that a mesh axis runs over, the one named last changes fastest.
Arguments:
- prior_realizations: bfloat16 [64, 73, 49152], P('member', None, 'space'), may hold values from -6 to 6
- expand_projection_matrix: bfloat16 [2, 512, 73], replicated, may hold values from -0.75 to 0.75
- contract_projection_matrix: bfloat16 [2, 73, 512], replicated, may hold values from -0.25 to 0.25
- obs_site: int32 [128, 512], P(('member', 'space')), may hold values from 0 to 46719
- obs_count: int32 [128], P(('member', 'space')), may hold values from 128 to 512, as said below
- obs_value: float32 [128, 512], P(('member', 'space')), may hold values from -5 to 5
- obs_weight: float32 [128, 512], P(('member', 'space')), may hold values from 0.05 to 1
Outputs:
- increments: bfloat16 [64, 73, 49152], P('member', None, 'space')
Inputs may be any that keep to these rules, and one draw needn't show every extreme that they name: `obs_count`: in every draw some tile has all 512 slots live.
All inputs are finite; a program needn't handle non-finite values.
Results may differ from a plain program's by a relative error of at most 0.0072.
Values may be sent and summed in bfloat16 or wider, within the bound.
A program may use at most 128 MiB of HBM per device.

v0:
```python
import jax
import jax.numpy as jnp
from jax import lax
from jax.sharding import PartitionSpec as P

HALO = 128


def with_halo(cells, sides, width):
    for axis, dim in sides:
        count = lax.axis_size(axis)
        ends = count - 1
        head = lax.slice_in_dim(cells, 0, width, axis=dim)
        tail = lax.slice_in_dim(cells, cells.shape[dim] - width, cells.shape[dim], axis=dim)
        cells = jnp.concatenate(
            [
                lax.ppermute(tail, axis, [(i, (i + 1) % count) for i in range(ends)]),
                cells,
                lax.ppermute(head, axis, [((i + 1) % count, i) for i in range(ends)]),
            ],
            axis=dim,
        )
    return cells


def march_one_interval(fields, expand_projection_matrix, contract_projection_matrix):
    current = fields.astype(jnp.float32)
    for layer_idx in range(expand_projection_matrix.shape[0]):
        center = current - jnp.mean(current, axis=1, keepdims=True)
        spread = jnp.mean(center * center, axis=1, keepdims=True)
        normed = (center * lax.rsqrt(spread + 1e-06)).astype(jnp.bfloat16)
        lifted = jnp.einsum(
            "hc,gcn->ghn",
            expand_projection_matrix[layer_idx],
            normed,
            preferred_element_type=jnp.float32,
        )
        hidden = jax.nn.gelu(lifted).astype(jnp.bfloat16)
        current = current + jnp.einsum(
            "ch,ghn->gcn",
            contract_projection_matrix[layer_idx],
            hidden,
            preferred_element_type=jnp.float32,
        )
    return current.astype(jnp.bfloat16)


def live_mask(place_row, live_count, tile_pos, tile_total, tile_len, margin):
    strip_spot = place_row % (tile_len + 2 * margin)
    slot_live = jnp.arange(place_row.shape[0], dtype=jnp.int32) < live_count
    low_edge = (strip_spot < margin) & (tile_pos == 0)
    high_edge = (strip_spot >= margin + tile_len) & (tile_pos == tile_total - 1)
    return slot_live & jnp.logical_not(low_edge) & jnp.logical_not(high_edge)


def analyse(observed, own_cells, value_row, weight_row, live_slots):
    members = observed.shape[0]
    highest = lax.Precision.HIGHEST
    obs_mean = jnp.mean(observed, axis=0)
    spread = observed - obs_mean
    departure = value_row - obs_mean
    rate = jnp.where(live_slots, weight_row, jnp.zeros_like(weight_row))
    scaled = spread * rate
    gram_matrix = jnp.dot(scaled, spread.T, precision=highest)
    drive = jnp.dot(scaled, departure, precision=highest)
    system = gram_matrix + (members - 1) * jnp.eye(members, dtype=jnp.float32)
    factor = jnp.linalg.cholesky(system)
    right_side = jnp.concatenate([drive[:, None], gram_matrix], axis=1)
    first_pass = lax.linalg.triangular_solve(factor, right_side, left_side=True, lower=True)
    solved = lax.linalg.triangular_solve(
        factor, first_pass, left_side=True, lower=True, transpose_a=True
    )
    mixing = solved[:, :1] - 0.5 * solved[:, 1:]
    field_f = own_cells.astype(jnp.float32)
    anomaly = field_f - jnp.mean(field_f, axis=0, keepdims=True)
    return jnp.einsum("jk,jcn->kcn", mixing, anomaly, precision=highest).astype(jnp.bfloat16)


def local(
    prior_realizations,
    expand_projection_matrix,
    contract_projection_matrix,
    obs_site,
    obs_count,
    obs_value,
    obs_weight,
):
    outgoing = lax.map(
        lambda lone_realization: march_one_interval(
            lone_realization[None], expand_projection_matrix, contract_projection_matrix
        )[0],
        prior_realizations,
    )
    tiled = lax.all_to_all(outgoing, "member", split_axis=2, concat_axis=0, tiled=True)
    members, channels, tile_len = tiled.shape
    margin = HALO
    strip_len = tile_len + 2 * margin
    tile_pos = lax.axis_index("member")
    tile_total = lax.axis_size("member")
    place_row = obs_site[0]
    live_slots = live_mask(place_row, obs_count[0], tile_pos, tile_total, tile_len, margin)
    strip_full = with_halo(tiled, (("member", 2),), margin)
    observed = jnp.take(
        strip_full.reshape(members, channels * strip_len), place_row, axis=1
    ).astype(jnp.float32)
    increment = analyse(observed, tiled, obs_value[0], obs_weight[0], live_slots)
    return lax.all_to_all(increment, "member", split_axis=0, concat_axis=2, tiled=True)


def solution(mesh):
    in_specs = (
        P("member", None, "space"),
        P(),
        P(),
        P(("member", "space"), None),
        P(("member", "space")),
        P(("member", "space"), None),
        P(("member", "space"), None),
    )
    out_specs = P("member", None, "space")
    return jax.shard_map(local, mesh=mesh, in_specs=in_specs, out_specs=out_specs, check_vma=False)
```

profile of v0, /device:TPU:0, one launch (start us, length us, event | category | flops | bytes accessed | tf_op | source)
XLA Modules:
  0.0 357.1 jit_solution(6895044969392270999)
XLA Ops:
  0.0 5.9 %copy.34 = bf16[2,73,12288]{2,1,0:T(8,128)(2,1)} copy(bf16[2,73,12288]{2,0,1:T(2,128)(2,1)} %param.9) | data formatting | bytes 7176192 | tf_op jit(solution)/shard_map/while | solution.py:88
  5.9 0.0 copy-done.1
  6.0 0.0 copy-done.2
  6.0 67.2 %while.10 = (s32[]{:T(128)}, bf16[2,73,12288]{2,1,0:T(8,128)(2,1)}, bf16[2,73,12288]{2,1,0:T(8,128)(2,1)}, bf16[2,512,73]{1,2,0:T(8,128)(2,1)S(1)}, bf16[2,73,512]{2,1,0:T(8,128)(2,1)S(1)}, /*index=5*/s32[]{:T(128)}) while((s32[]{:T(128)}, bf16[2,73,12288]{2,1,0:T(8,128)(2,1)}, bf16[2,73,12288]{2,1,0:T(8,128)(2,1)}, ...), condition=%wide.region_5.6_spmd, body=%wide.region_0.5_spmd.sunk | while | flops 3806318592 | bytes 24708184 | solution.py:88
  6.0 1.9 convert_reduce_fusion.4
  7.9 2.2 fusion.116
  10.1 13.8 %fusion.117 = (f32[12288]{0:T(1024)S(1)}, f32[1,73,12288]{2,1,0:T(8,128)}) fusion(bf16[2,73,512]{2,1,0:T(8,128)(2,1)S(1)} %get-tuple-element.120, f32[12288]{0:T(1024)S(1)} %add_rsqrt_fusion.4, f32[12288]{0:T(1024)S(1)} %broadcast_multiply_fusion.6, bf16[2,73,12288]{2,1,0:T(8,128)(2,1)} %get-tuple-element.118, s32[]{:T(128)S(6)} %copy.52, ...), kind=kOutput, calls=%fused_computation.115.clone.1 | convolution fusion | flops 1899995136 | bytes 7488512 | tf_op jit(solution)/shard_map/while/body/eval_jaxpr/ch,ghn->gcn/dot_general | solution.py:39
  23.9 2.6 multiply_reduce_fusion.2
  26.6 13.1 %fusion.118 = bf16[2,73,12288]{2,1,0:T(8,128)(2,1)} fusion(bf16[2,73,12288]{2,1,0:T(8,128)(2,1)} %get-tuple-element.111, s32[]{:T(128)S(6)} %copy.52, f32[1,73,12288]{2,1,0:T(8,128)} %get-tuple-element.102, f32[12288]{0:T(1024)S(1)} %add_rsqrt_fusion.5, f32[12288]{0:T(1024)S(1)} %broadcast_multiply_fusion.7, ...), kind=kOutput, calls=%fused_computation.26.clone.1 | convolution fusion | flops 1898213376 | bytes 9404420 | tf_op jit(solution)/shard_map/while/body/eval_jaxpr/ch,ghn->gcn/dot_general | solution.py:39
  39.7 1.9 convert_reduce_fusion.4
  41.6 2.2 fusion.116
  43.8 13.7 %fusion.117 = (f32[12288]{0:T(1024)S(1)}, f32[1,73,12288]{2,1,0:T(8,128)}) fusion(bf16[2,73,512]{2,1,0:T(8,128)(2,1)S(1)} %get-tuple-element.120, f32[12288]{0:T(1024)S(1)} %add_rsqrt_fusion.4, f32[12288]{0:T(1024)S(1)} %broadcast_multiply_fusion.6, bf16[2,73,12288]{2,1,0:T(8,128)(2,1)} %get-tuple-element.118, s32[]{:T(128)S(6)} %copy.52, ...), kind=kOutput, calls=%fused_computation.115.clone.1 | convolution fusion | flops 1899995136 | bytes 7488512 | tf_op jit(solution)/shard_map/while/body/eval_jaxpr/ch,ghn->gcn/dot_general | solution.py:39
  57.5 2.6 multiply_reduce_fusion.2
  60.1 13.1 %fusion.118 = bf16[2,73,12288]{2,1,0:T(8,128)(2,1)} fusion(bf16[2,73,12288]{2,1,0:T(8,128)(2,1)} %get-tuple-element.111, s32[]{:T(128)S(6)} %copy.52, f32[1,73,12288]{2,1,0:T(8,128)} %get-tuple-element.102, f32[12288]{0:T(1024)S(1)} %add_rsqrt_fusion.5, f32[12288]{0:T(1024)S(1)} %broadcast_multiply_fusion.7, ...), kind=kOutput, calls=%fused_computation.26.clone.1 | convolution fusion | flops 1898213376 | bytes 9404420 | tf_op jit(solution)/shard_map/while/body/eval_jaxpr/ch,ghn->gcn/dot_general | solution.py:39
  73.2 14.0 %copy.37 = bf16[2,73,12288]{1,0,2:T(2,128)(2,1)} copy(bf16[2,73,12288]{2,1,0:T(8,128)(2,1)} %get-tuple-element.32) | data formatting | bytes 7176192 | tf_op jit(solution)/shard_map/while | solution.py:88
  87.2 9.0 %all-to-all-start = ((bf16[2,73,12288]{1,0,2:T(2,128)(2,1)}), bf16[2,73,12288]{1,0,2:T(2,128)(2,1)}, u32[]{:S(2)}, u32[]{:S(2)}) async-start(bf16[2,73,12288]{1,0,2:T(2,128)(2,1)} %copy.37), calls=%async_computation | async-start | bytes 12582912 | tf_op jit(solution)/shard_map/all_to_all | solution.py:94
  96.9 86.4 %all-to-all-done = bf16[2,73,12288]{1,0,2:T(2,128)(2,1)} async-done(((bf16[2,73,12288]{1,0,2:T(2,128)(2,1)}), bf16[2,73,12288]{1,0,2:T(2,128)(2,1)}, u32[]{:S(2)}, u32[]{:S(2)}) %all-to-all-start) | async-done | bytes 3588128 | tf_op jit(solution)/shard_map/all_to_all | solution.py:94
  183.3 10.9 %copy.47 = bf16[2,73,32,384]{3,2,0,1:T(8,128)(2,1)} copy(bf16[2,73,32,384]{1,0,3,2:T(2,128)(2,1)} %bitcast.19) | data formatting | bytes 7176192 | tf_op jit(solution)/shard_map/all_to_all | solution.py:94
  194.2 7.6 %copy.39 = bf16[32,2,73,384]{3,1,0,2:T(2,128)(2,1)} copy(bf16[32,2,73,384]{3,0,1,2:T(8,128)(2,1)} %bitcast.141) | data formatting | bytes 7176192 | tf_op jit(solution)/shard_map/all_to_all | solution.py:94
  201.8 8.5 %all_to_all.29 = bf16[64,73,384]{2,0,1:T(8,128)(2,1)} reshape(bf16[32,2,73,384]{3,1,0,2:T(2,128)(2,1)} %copy.39) | data formatting | bytes 7176192 | tf_op jit(solution)/shard_map/all_to_all | solution.py:94
  210.4 2.3 fusion.100
  212.7 1.3 collective-permute-start.1
  214.0 4.6 %collective-permute-start = (bf16[64,73,128]{2,0,1:T(8,128)(2,1)S(1)}, bf16[64,73,128]{2,0,1:T(8,128)(2,1)S(1)}, u32[]{:S(2)}, u32[]{:S(2)}) collective-permute-start(bf16[64,73,128]{2,0,1:T(8,128)(2,1)S(1)} %get-tuple-element.65), channel_id=1, source_target_pairs={{0,4},{4,8},{8,12},{12,16},{16,20},{20,24},{24,28},{28,32},{32,36}... | collective-permute-start | bytes 3588104 | tf_op jit(solution)/shard_map/ppermute | solution.py:17
  218.6 0.0 copy-done.3
  218.7 0.0 copy-done.4
  218.7 3.1 convert_reduce_fusion.1
  221.8 19.7 %collective-permute-done.1 = bf16[64,73,128]{2,0,1:T(8,128)(2,1)S(1)} collective-permute-done((bf16[64,73,128]{2,0,1:T(8,128)(2,1)S(1)}, bf16[64,73,128]{2,0,1:T(8,128)(2,1)S(1)}, u32[]{:S(2)}, u32[]{:S(2)}) %collective-permute-start.1) | collective-permute-done | bytes 1196064 | tf_op jit(solution)/shard_map/ppermute | solution.py:19
  241.5 1.2 collective-permute-done
  242.7 0.0 copy-done
  242.7 3.2 pad_maximum_fusion
  245.9 12.2 %copy.40 = bf16[64,73,640]{0,2,1:T(8,128)(2,1)} copy(bf16[64,73,640]{2,0,1:T(8,128)(2,1)} %pad_maximum_fusion) | data formatting | bytes 11960320 | tf_op jit(solution)/shard_map/concatenate | solution.py:15
  258.1 7.0 %gather_fusion = bf16[512,64]{1,0:T(8,128)(2,1)S(1)} fusion(bf16[64,46720]{0,1:T(8,128)(2,1)} %bitcast.143, s32[1024]{0:T(1024)S(1)} %pad_clamp_fusion), kind=kCustom, calls=%fused_computation | custom fusion | bytes 133120 | tf_op jit(solution)/shard_map/jit(_take)/gather | solution.py:103
  265.1 0.2 convert_reduce_fusion.2
  265.3 1.0 fusion.71
  266.4 0.9 convolution_bitcast_fusion.2
  267.2 0.1 copy.41
  267.3 5.8 %cholesky.16 = f32[64,64]{1,0:T(8,128)S(1)} custom-call(f32[64,64]{1,0:T(8,128)S(1)} %fusion.89), custom_call_target="Cholesky" | custom-call | tf_op jit(solution)/shard_map/jit(cholesky)/cholesky | solution.py:67
  273.2 0.6 compare_reduce_fusion
  273.9 0.7 fusion.77
  274.5 4.9 %custom-call.8 = f32[1,64,64]{1,2,0:T(8,128)S(1)} custom-call(f32[1,64,64]{2,1,0:T(8,128)S(1)} %fusion.77), custom_call_target="InvertDiagBlocksLowerTriangular" | custom-call | tf_op jit(solution)/shard_map/triangular_solve | solution.py:70
  279.4 0.3 fusion.81
  279.7 0.2 fusion.85
  279.9 0.1 slice_reduce_fusion
  280.0 8.1 %fusion.68 = bf16[64,73,384]{2,0,1:T(8,128)(2,1)S(1)} fusion(bf16[64,73,384]{2,0,1:T(8,128)(2,1)} %all_to_all.29, f32[73,384]{1,0:T(8,128)S(1)} %broadcast_multiply_fusion.2, f32[64,65]{1,0:T(8,128)S(1)} %fusion.85, f32[64]{0:T(128)S(1)} %slice_reduce_fusion), kind=kOutput, calls=%fused_computation.69 | convolution fusion | flops 1383219200 | bytes 7305216 | tf_op jit(solution)/shard_map/jk,jcn->kcn/dot_general | solution.py:76
  288.0 2.2 copy.44
  290.2 55.7 %all_to_all.36 = bf16[64,73,384]{2,1,0:T(8,128)(2,1)S(1)} all-to-all(bf16[64,73,384]{2,1,0:T(8,128)(2,1)S(1)} %copy.44), channel_id=1, replica_groups=mesh['member'=32,'space'=4] {'member'}, dimensions={0} | all-to-all | bytes 7176192 | tf_op jit(solution)/shard_map/all_to_all | solution.py:107
  345.9 3.1 copy.45
  348.9 8.2 %all_to_all.33 = bf16[2,73,12288]{2,0,1:T(2,128)(2,1)} reshape(bf16[2,73,32,384]{3,2,0,1:T(8,128)(2,1)} %copy.45) | data formatting | bytes 7176192 | tf_op jit(solution)/shard_map/all_to_all | solution.py:107
  (26 shorter events, 0.3 us)
Async XLA Ops:
  0.0 6.0 %copy-start.1 = (bf16[2,512,73]{1,0,2:T(2,128)(2,1)S(1)}, bf16[2,512,73]{1,0,2:T(2,128)(2,1)}, u32[]{:S(2)}) copy-start(bf16[2,512,73]{1,0,2:T(2,128)(2,1)} %param.10) | copy-start | bytes 448516
  0.0 6.0 %copy-start.2 = (bf16[2,73,512]{2,0,1:T(2,128)(2,1)S(1)}, bf16[2,73,512]{2,0,1:T(2,128)(2,1)}, u32[]{:S(2)}) copy-start(bf16[2,73,512]{2,0,1:T(2,128)(2,1)} %param.11) | copy-start | bytes 448516
  87.2 96.0 %all-to-all-start = ((bf16[2,73,12288]{1,0,2:T(2,128)(2,1)}), bf16[2,73,12288]{1,0,2:T(2,128)(2,1)}, u32[]{:S(2)}, u32[]{:S(2)}) async-start(bf16[2,73,12288]{1,0,2:T(2,128)(2,1)} %copy.37), calls=%async_computation | async-start | bytes 12582912 | tf_op jit(solution)/shard_map/all_to_all | solution.py:94
  210.4 8.2 %copy-start.3 = (s32[1,512]{1,0:T(1,128)S(1)}, s32[1,512]{1,0:T(1,128)}, u32[]{:S(2)}) copy-start(s32[1,512]{1,0:T(1,128)} %param.12) | copy-start | bytes 6148
  210.4 8.3 %copy-start.4 = (f32[1,512]{1,0:T(1,128)S(1)}, f32[1,512]{1,0:T(1,128)}, u32[]{:S(2)}) copy-start(f32[1,512]{1,0:T(1,128)} %param.15) | copy-start | bytes 6148
  210.4 32.3 %copy-start = (bf16[64,73,384]{2,0,1:T(8,128)(2,1)S(1)}, bf16[64,73,384]{2,0,1:T(8,128)(2,1)}, u32[]{:S(2)}) copy-start(bf16[64,73,384]{2,0,1:T(8,128)(2,1)} %all_to_all.29) | copy-start | bytes 10764292
  212.7 28.8 %collective-permute-start.1 = (bf16[64,73,128]{2,0,1:T(8,128)(2,1)S(1)}, bf16[64,73,128]{2,0,1:T(8,128)(2,1)S(1)}, u32[]{:S(2)}, u32[]{:S(2)}) collective-permute-start(bf16[64,73,128]{2,0,1:T(8,128)(2,1)S(1)} %get-tuple-element.66), channel_id=1, source_target_pairs={{4,0},{8,4},{12,8},{16,12},{20,16},{24,20},{28,24},{32,28},{36,32}... | collective-permute-start | bytes 3588104 | tf_op jit(solution)/shard_map/ppermute | solution.py:19
  214.0 28.7 %collective-permute-start = (bf16[64,73,128]{2,0,1:T(8,128)(2,1)S(1)}, bf16[64,73,128]{2,0,1:T(8,128)(2,1)S(1)}, u32[]{:S(2)}, u32[]{:S(2)}) collective-permute-start(bf16[64,73,128]{2,0,1:T(8,128)(2,1)S(1)} %get-tuple-element.65), channel_id=1, source_target_pairs={{0,4},{4,8},{8,12},{12,16},{16,20},{20,24},{24,28},{28,32},{32,36}... | collective-permute-start | bytes 3588104 | tf_op jit(solution)/shard_map/ppermute | solution.py:17
  245.9 19.4 %copy-start.5 = (f32[1,512]{1,0:T(1,128)S(1)}, f32[1,512]{1,0:T(1,128)}, u32[]{:S(2)}) copy-start(f32[1,512]{1,0:T(1,128)} %param.14) | copy-start | bytes 6148
where the time goes:
time: 359 us; the launch traced here: 357 us
  waiting for transfers between devices  107 us (30%)
  local copies, waits for them, and re-layouts  82.2 us (23%)
  matrix products  64.1 us (18%)
  blocking collectives  55.7 us (16%)
  other arithmetic  32 us (9%)
  starting transfers between devices  14.9 us (4%)
    all_to_all x1, waiting for transfers between devices, local(): lax.all_to_all(outgoing, 'member', split_axis=2, concat_axis=0, tiled=True)  86.4 us
    all_to_all x1, blocking collectives, local(): lax.all_to_all(increment, 'member', split_axis=0, concat_axis=2, tiled=True)  55.7 us
    dot_general x4, matrix products, march_one_interval(): jnp.einsum('ch,ghn->gcn', contract_projection_matrix[layer_idx], hidden,...  53.7 us
    all_to_all x3, local copies, waits for them, and re-layouts, local(): lax.all_to_all(outgoing, 'member', split_axis=2, concat_axis=0, tiled=True)  27.1 us
    while x4, local copies, waits for them, and re-layouts, local(): lax.map(lambda lone_realization: march_one_interval(lone_realization[None...  20 us
    ppermute x1, waiting for transfers between devices, with_halo(): lax.ppermute(head, axis, [((i + 1) % count, i) for i in range(ends)])  19.7 us
    concatenate x1, local copies, waits for them, and re-layouts, with_halo(): jnp.concatenate([lax.ppermute(tail, axis, [(i, (i + 1) % count) for i in...  12.2 us
    all_to_all x2, local copies, waits for them, and re-layouts, local(): lax.all_to_all(increment, 'member', split_axis=0, concat_axis=2, tiled=True)  11.2 us
  transfers between devices with their start and end apart: 3, of which 3 were waited for; matrix products, arithmetic and copies ran while one was open for 1% of the time, Pallas kernels for 0%

commit v1 on v0

v1 whole, which is shorter than its diff:
```python
import functools
import math

import jax
import jax.numpy as jnp
from jax import lax
from jax.experimental import pallas as pl
from jax.experimental.pallas import tpu as pltpu
from jax.sharding import PartitionSpec as P

MESH = pl.DeviceIdType.MESH
F32 = jnp.float32
BF16 = jnp.bfloat16

CH = 73
TILE = 384
HALO = 128
STRIP = TILE + 2 * HALO
SLOTS = 512
MEMBERS = 64
PEERS = 32
PITCH = 80
LANES = 128
BLOCKS = TILE // LANES
ROWS = 448
GELU_A = math.sqrt(2.0 / math.pi)
GELU_B = GELU_A * 0.044715


def peer_of(me, step):
    off = lax.rem(step * ORDER, PEERS)
    x = lax.rem(lax.rem(me, 4) + lax.rem(off, 4), 4)
    y = lax.rem(lax.rem(me // 4, 4) + lax.rem(off // 4, 4), 4)
    z = lax.rem(me // 16 + off // 16, 2)
    return z * 16 + y * 4 + x


ORDER = 25


def layer(x, w_up, w_down):
    mean = jnp.sum(x, axis=0, keepdims=True) * (1.0 / CH)
    center = x - mean
    var = jnp.sum(center * center, axis=0, keepdims=True) * (1.0 / CH)
    normed = (center * lax.rsqrt(var + 1e-06)).astype(BF16)
    lifted = jnp.dot(w_up, normed, preferred_element_type=F32)
    bend = jnp.tanh(lifted * (GELU_A + GELU_B * (lifted * lifted)))
    half = 0.5 * lifted
    hidden = (half + half * bend).astype(BF16)
    return x + jnp.dot(w_down, hidden, preferred_element_type=F32)


def pack_message(blocks, msg, slot):
    for b, block in enumerate(blocks):
        msg[slot, b * 64 : b * 64 + 64, :] = block[:64].astype(BF16)
    for b in range(0, 2 * BLOCKS, 2):
        pair = jnp.concatenate([blocks[b][64:72], blocks[b + 1][64:72]], axis=0)
        msg[slot, 384 + 8 * b : 400 + 8 * b, :] = pair.astype(BF16)
    last = [block[72:73] for block in blocks]
    last.append(jnp.zeros((16 - 2 * BLOCKS, LANES), F32))
    msg[slot, 432:448, :] = jnp.concatenate(last, axis=0).astype(BF16)


def kernel(
    prior,
    w_up,
    w_down,
    site,
    count,
    value,
    weight,
    out,
    msg1,
    got1,
    msg2,
    got2,
    state,
    code_own,
    code_out,
    code_in,
    smem_own,
    smem_in,
    obs_own,
    obs_out,
    obs_in,
    send1,
    recv1,
    send2,
    recv2,
    near_send,
    near_recv,
    local_sem,
):
    me = lax.axis_index("member")
    left = lax.rem(me + PEERS - 1, PEERS)
    right = lax.rem(me + 1, PEERS)

    barrier = pltpu.get_barrier_semaphore()

    def greet(step, carry):
        pl.semaphore_signal(
            barrier, inc=1, device_id={"member": peer_of(me, step)}, device_id_type=MESH
        )
        return carry

    lax.fori_loop(1, PEERS, greet, 0)

    sites = site[...]
    channel = ((sites >> 7) * 6554) >> 15
    spot = sites - channel * STRIP
    slot_id = lax.broadcasted_iota(jnp.int32, (1, SLOTS), 1)

    def code(cell):
        row = (cell >> 7) * (MEMBERS * PITCH) + channel
        return row * LANES + ((slot_id - cell) & (LANES - 1))

    code_own[...] = code(jnp.clip(spot - HALO, 0, TILE - 1))
    code_out[0] = code(jnp.minimum(spot, HALO - 1) + (TILE - HALO))
    code_out[1] = code(jnp.maximum(spot - (HALO + TILE), 0))

    own_codes = pltpu.make_async_copy(code_own, smem_own, local_sem.at[0])
    own_codes.start()

    pl.semaphore_wait(barrier, PEERS - 1)

    def near_copy(src, dst, sem, target):
        return pltpu.make_async_remote_copy(
            src_ref=src,
            dst_ref=dst,
            send_sem=near_send.at[sem],
            recv_sem=near_recv.at[sem],
            device_id={"member": target},
            device_id_type=MESH,
        )

    code_left = near_copy(code_out.at[0], code_in.at[0], 0, left)
    code_right = near_copy(code_out.at[1], code_in.at[1], 1, right)
    code_left.start()
    code_right.start()

    def exchange(msg, got, send, recv, target, source):
        return pltpu.make_async_remote_copy(
            src_ref=msg.at[target],
            dst_ref=got.at[source],
            send_sem=send.at[target],
            recv_sem=recv.at[source],
            device_id={"member": target},
            device_id_type=MESH,
        )

    def forecast(target):
        start = pl.multiple_of(target * TILE, TILE)
        x = jnp.concatenate(
            [prior[m, :, pl.ds(start, TILE)].astype(F32) for m in range(2)], axis=1
        )
        for l in range(2):
            x = layer(x, w_up[l], w_down[l])
        pack_message(
            [x[:, b * LANES : (b + 1) * LANES] for b in range(2 * BLOCKS)], msg1, target
        )

    def forecast_step(i, carry):
        target = peer_of(me, i)
        forecast(target)
        exchange(msg1, got1, send1, recv1, target, me).start()
        return carry

    lax.fori_loop(1, PEERS, forecast_step, 0)
    forecast(me)
    own_tile = pltpu.make_async_copy(msg1.at[me], got1.at[me], local_sem.at[1])
    own_tile.start()

    code_left.wait()
    code_right.wait()
    in_codes = pltpu.make_async_copy(code_in, smem_in, local_sem.at[2])
    in_codes.start()

    def unpack(source):
        tail = got1[source, 384:448, :].astype(F32)
        for m in range(2):
            for j in range(BLOCKS):
                b = m * BLOCKS + j
                base = pl.multiple_of(j * (MEMBERS * PITCH) + (2 * source + m) * PITCH, 8)
                state[pl.ds(base, 64), :] = got1[source, b * 64 : b * 64 + 64, :].astype(F32)
                state[pl.ds(base + 64, 8), :] = tail[8 * b : 8 * b + 8]
                state[pl.ds(base + 72, 1), :] = tail[48 + b : 49 + b]

    own_tile.wait()
    unpack(me)

    def receive_step(i, carry):
        source = source_of(me, i)
        exchange(msg1, got1, send1, recv1, source, source).wait_recv()
        unpack(source)
        return carry

    lax.fori_loop(1, PEERS, receive_step, 0)

    own_codes.wait()
    in_codes.wait()

    lane = lax.broadcasted_iota(jnp.int32, (MEMBERS, LANES), 1)

    def gather(read_code, group):
        def one(p, acc):
            word = read_code(group * LANES + p)
            slab = state[pl.ds(word >> 7, MEMBERS, stride=PITCH), :]
            moved = pltpu.roll(slab, word & (LANES - 1), 1)
            return jnp.where(lane == p, moved, acc)

        return lax.fori_loop(
            0, LANES, one, jnp.zeros((MEMBERS, LANES), F32), unroll=8
        )

    for g in range(SLOTS // LANES):
        span = slice(g * LANES, (g + 1) * LANES)
        obs_out[0, :, span] = gather(lambda p: smem_in[1, 0, p], g).astype(BF16)
        obs_out[1, :, span] = gather(lambda p: smem_in[0, 0, p], g).astype(BF16)
    obs_left = near_copy(obs_out.at[0], obs_in.at[0], 2, left)
    obs_right = near_copy(obs_out.at[1], obs_in.at[1], 3, right)
    obs_left.start()
    obs_right.start()
    for g in range(SLOTS // LANES):
        span = slice(g * LANES, (g + 1) * LANES)
        obs_own[:, span] = gather(lambda p: smem_own[0, p], g)
    obs_left.wait()
    obs_right.wait()

    below = spot < HALO
    above = spot >= HALO + TILE
    observed = jnp.where(
        below,
        obs_in[1].astype(F32),
        jnp.where(above, obs_in[0].astype(F32), obs_own[...]),
    )
    live = slot_id < count[0]
    live = live & jnp.logical_not(below & (me == 0))
    live = live & jnp.logical_not(above & (me == PEERS - 1))
    rate = jnp.where(live, weight[...], 0.0)
    obs_mean = jnp.sum(observed, axis=0, keepdims=True) * (1.0 / MEMBERS)
    spread = observed - obs_mean
    departure = value[...] - obs_mean
    scaled = spread * rate
    right_side = jnp.concatenate(
        [spread, jnp.broadcast_to(departure, (MEMBERS, SLOTS))], axis=0
    )
    gram_drive = lax.dot_general(
        scaled,
        right_side,
        (((1,), (1,)), ((), ())),
        precision=lax.Precision.HIGHEST,
        preferred_element_type=F32,
    )
    row_id = lax.broadcasted_iota(jnp.int32, (MEMBERS, 2 * MEMBERS), 0)
    col_id = lax.broadcasted_iota(jnp.int32, (MEMBERS, 2 * MEMBERS), 1)
    swapped = pltpu.roll(gram_drive, MEMBERS, 1)
    system = jnp.where(
        col_id < MEMBERS,
        jnp.where(row_id == col_id, gram_drive + (MEMBERS - 1.0), gram_drive),
        gram_drive - 0.5 * swapped,
    )
    for j in range(MEMBERS):
        pivot_row = system[j : j + 1, :]
        pivot_row = pivot_row / system[j : j + 1, j : j + 1]
        column = system[:, j : j + 1]
        system = jnp.where(row_id == j, pivot_row, system - column * pivot_row)
    mixing = system[:, MEMBERS:]
    mixing = mixing - jnp.sum(mixing, axis=0, keepdims=True) * (1.0 / MEMBERS)
    mixing_t = mixing.T
    coarse = mixing_t.astype(BF16)
    fine = (mixing_t - coarse.astype(F32)).astype(BF16)
    mixer = jnp.concatenate([coarse, fine], axis=1)

    def mix(c, carry):
        rows = [pl.ds(j * (MEMBERS * PITCH) + c, MEMBERS, stride=PITCH) for j in range(BLOCKS)]
        slab = jnp.concatenate([state[r, :] for r in rows], axis=1).astype(BF16)
        mixed = jnp.dot(
            mixer, jnp.concatenate([slab, slab], axis=0), preferred_element_type=F32
        )
        for j, r in enumerate(rows):
            state[r, :] = mixed[:, j * LANES : (j + 1) * LANES]
        return carry

    lax.fori_loop(0, CH, mix, 0)

    def pack_for(target):
        blocks = []
        for m in range(2):
            for j in range(BLOCKS):
                base = pl.multiple_of(j * (MEMBERS * PITCH) + (2 * target + m) * PITCH, 8)
                blocks.append(state[pl.ds(base, CH), :])
        pack_message(blocks, msg2, target)

    def send_step(i, carry):
        target = peer_of(me, i)
        pack_for(target)
        exchange(msg2, got2, send2, recv2, target, me).start()
        return carry

    lax.fori_loop(1, PEERS, send_step, 0)
    pack_for(me)

    def place(got, source):
        start = pl.multiple_of(source * TILE, TILE)
        tail = got[source, 384:448, :].astype(F32)
        for m in range(2):
            for j in range(BLOCKS):
                b = m * BLOCKS + j
                span = pl.ds(pl.multiple_of(start + j * LANES, LANES), LANES)
                out[m, 0:64, span] = got[source, b * 64 : b * 64 + 64, :]
                rest = jnp.concatenate([tail[8 * b : 8 * b + 8], tail[48 + b : 49 + b]], axis=0)
                out[m, 64:CH, span] = rest.astype(BF16)

    place(msg2, me)

    def place_step(i, carry):
        source = source_of(me, i)
        exchange(msg2, got2, send2, recv2, source, source).wait_recv()
        place(got2, source)
        return carry

    lax.fori_loop(1, PEERS, place_step, 0)

    def sent_step(i, carry):
        target = peer_of(me, i)
        exchange(msg1, got1, send1, recv1, target, me).wait_send()
        exchange(msg2, got2, send2, recv2, target, me).wait_send()
        return carry

    lax.fori_loop(1, PEERS, sent_step, 0)


def source_of(me, step):
    off = lax.rem(step * ORDER, PEERS)
    x = lax.rem(lax.rem(me, 4) + 4 - lax.rem(off, 4), 4)
    y = lax.rem(lax.rem(me // 4, 4) + 4 - lax.rem(off // 4, 4), 4)
    z = lax.rem(me // 16 + off // 16, 2)
    return z * 16 + y * 4 + x


def local(prior, w_up, w_down, site, count, value, weight):
    vmem = pl.BlockSpec(memory_space=pltpu.VMEM)
    smem = pl.BlockSpec(memory_space=pltpu.SMEM)
    return pl.pallas_call(
        kernel,
        out_shape=jax.ShapeDtypeStruct(prior.shape, BF16),
        in_specs=[vmem, vmem, vmem, vmem, smem, vmem, vmem],
        out_specs=vmem,
        scratch_shapes=[
            pltpu.VMEM((PEERS, ROWS, LANES), BF16),
            pltpu.VMEM((PEERS, ROWS, LANES), BF16),
            pltpu.VMEM((PEERS, ROWS, LANES), BF16),
            pltpu.VMEM((PEERS, ROWS, LANES), BF16),
            pltpu.VMEM((BLOCKS * MEMBERS * PITCH, LANES), F32),
            pltpu.VMEM((1, SLOTS), jnp.int32),
            pltpu.VMEM((2, 1, SLOTS), jnp.int32),
            pltpu.VMEM((2, 1, SLOTS), jnp.int32),
            pltpu.SMEM((1, SLOTS), jnp.int32),
            pltpu.SMEM((2, 1, SLOTS), jnp.int32),
            pltpu.VMEM((MEMBERS, SLOTS), F32),
            pltpu.VMEM((2, MEMBERS, SLOTS), BF16),
            pltpu.VMEM((2, MEMBERS, SLOTS), BF16),
            pltpu.SemaphoreType.DMA((PEERS,)),
            pltpu.SemaphoreType.DMA((PEERS,)),
            pltpu.SemaphoreType.DMA((PEERS,)),
            pltpu.SemaphoreType.DMA((PEERS,)),
            pltpu.SemaphoreType.DMA((4,)),
            pltpu.SemaphoreType.DMA((4,)),
            pltpu.SemaphoreType.DMA((3,)),
        ],
        compiler_params=pltpu.CompilerParams(
            collective_id=0, has_side_effects=True, vmem_limit_bytes=56 << 20
        ),
    )(prior, w_up, w_down, site, count, value, weight)


def solution(mesh):
    in_specs = (
        P("member", None, "space"),
        P(),
        P(),
        P(("member", "space"), None),
        P(("member", "space")),
        P(("member", "space"), None),
        P(("member", "space"), None),
    )
    return jax.shard_map(
        local,
        mesh=mesh,
        in_specs=in_specs,
        out_specs=P("member", None, "space"),
        check_vma=False,
    )
```

time: 359 us -> 189 us (0.53)
  Pallas kernels: 0 us -> 171 us
  waiting for transfers between devices: 107 us -> 0 us
  local copies, waits for them, and re-layouts: 82.2 us -> 17 us
  matrix products: 64.1 us -> 0 us
  blocking collectives: 55.7 us -> 0 us
  other arithmetic: 32 us -> 0 us
  starting transfers between devices: 14.9 us -> 0 us
    pallas_call x0 -> x1, Pallas kernels: none -> 171 us  [local(): pl.pallas_call(kernel, out_shape=jax.ShapeDtypeStruct(prior.shape, BF16),...]
    all_to_all x1 -> x0, waiting for transfers between devices: 86.4 us -> none  [local(): lax.all_to_all(outgoing, 'member', split_axis=2, concat_axis=0, tiled=True)]
    dot_general x7 -> x0, matrix products: 63.7 us -> none  [the longest x4 53.7 us: march_one_interval(): jnp.einsum('ch,ghn->gcn', contract_projection_matrix[layer_idx], hidden,...]
    all_to_all x1 -> x0, blocking collectives: 55.7 us -> none  [local(): lax.all_to_all(increment, 'member', split_axis=0, concat_axis=2, tiled=True)]
    all_to_all x5 -> x0, local copies, waits for them, and re-layouts: 38.4 us -> none  [the longest x3 27.1 us: local(): lax.all_to_all(outgoing, 'member', split_axis=2, concat_axis=0, tiled=True)]
    ppermute x2 -> x0, waiting for transfers between devices: 20.9 us -> none  [the longest x1 19.7 us: with_halo(): lax.ppermute(head, axis, [((i + 1) % count, i) for i in range(ends)])]
    while x4 -> x0, local copies, waits for them, and re-layouts: 20 us -> none  [local(): lax.map(lambda lone_realization: march_one_interval(lone_realization[None...]
    reduce_sum x8 -> x0, other arithmetic: 16.6 us -> none  [the longest x4 9.5 us: march_one_interval(): spread = jnp.mean(center * center, axis=1, keepdims=True)]
  transfers between devices with their start and end apart: 3 -> 0, of which waited for: 3 -> 0; matrix products, arithmetic and copies ran while one was open for 1% -> 0% of each run, Pallas kernels for 0% -> 0%
where the time goes in v1:
time: 189 us
  Pallas kernels  171 us (90%)
  local copies, waits for them, and re-layouts  17 us (9%)
    pallas_call x1, Pallas kernels, local(): pl.pallas_call(kernel, out_shape=jax.ShapeDtypeStruct(prior.shape, BF16),...  171 us
    unnamed x3, local copies, waits for them, and re-layouts  9.28 us
    pallas_call x1, local copies, waits for them, and re-layouts, local(): pl.pallas_call(kernel, out_shape=jax.ShapeDtypeStruct(prior.shape, BF16),...  7.69 us

profile of v1, /device:TPU:0, one launch (start us, length us, event | category | flops | bytes accessed | tf_op | source)
XLA Modules:
  0.0 189.0 jit_solution(16512206767317333644)
XLA Ops:
  0.7 1.6 copy.10.w_down
  2.2 1.8 copy.9.w_up
  4.0 5.9 %copy.8.prior = bf16[2,73,12288]{2,1,0:T(8,128)(2,1)} copy(bf16[2,73,12288]{2,0,1:T(2,128)(2,1)} %param.7) | data formatting | bytes 7176192 | tf_op args[0]
  9.9 171.3 %shard_map.73 = bf16[2,73,12288]{2,1,0:T(8,128)(2,1)} custom-call(bf16[2,73,12288]{2,1,0:T(8,128)(2,1)} %copy.8.prior, bf16[2,512,73]{2,1,0:T(8,128)(2,1)} %copy.9.w_up, bf16[2,73,512]{2,1,0:T(8,128)(2,1)} %copy.10.w_down, s32[1,512]{1,0:T(1,128)} %site.1, s32[1]{0:T(128)S(6)} %copy.12.count, f32[1,512]{1,0:T(1,128)} %value.1, f32[1,512]{1,0:T(1,128)} %weight.1), custom_call_target="tpu_custom_call" | custom-call | tf_op jit(solution)/shard_map/pallas_call | solution.py:344
  181.3 7.7 %copy.11 = bf16[2,73,12288]{2,0,1:T(2,128)(2,1)} copy(bf16[2,73,12288]{2,1,0:T(8,128)(2,1)} %shard_map.73) | data formatting | bytes 7176192 | tf_op jit(solution)/shard_map/pallas_call | solution.py:344

commit v2 on v1

v2 whole, which is shorter than its diff:
```python
import functools
import math

import jax
import jax.numpy as jnp
from jax import lax
from jax.experimental import pallas as pl
from jax.experimental.pallas import tpu as pltpu
from jax.sharding import PartitionSpec as P

MESH = pl.DeviceIdType.MESH
F32 = jnp.float32
BF16 = jnp.bfloat16

CH = 73
TILE = 384
HALO = 128
STRIP = TILE + 2 * HALO
SLOTS = 512
MEMBERS = 64
PEERS = 32
FILL = 80
PAIR = 152
HID = 512
LANES = 128
BLOCKS = TILE // LANES
ORDER = 25
GROUP = 4
HALVES = 38
GELU_A = math.sqrt(2.0 / math.pi)
GELU_B = GELU_A * 0.044715


def peer_of(me, step):
    off = lax.rem(step * ORDER, PEERS)
    x = lax.rem(lax.rem(me, 4) + lax.rem(off, 4), 4)
    y = lax.rem(lax.rem(me // 4, 4) + lax.rem(off // 4, 4), 4)
    z = lax.rem(me // 16 + off // 16, 2)
    return z * 16 + y * 4 + x


def normalise(x):
    groups = x.reshape(PAIR // 8, 8, x.shape[1])

    def over_channels(group):
        group = group + pltpu.roll(group, 4, 0)
        return (group + pltpu.roll(group, 2, 0)) * (1.0 / CH)

    center = groups - over_channels(jnp.sum(groups, axis=0))[None]
    row = lax.broadcasted_iota(jnp.int32, center.shape[1:], 0)
    last = jnp.where(row < 2, center[PAIR // 8 - 1], 0.0)
    center = jnp.concatenate([center[: PAIR // 8 - 1], last[None]], axis=0)
    var = over_channels(jnp.sum(center * center, axis=0))
    return (center * lax.rsqrt(var + 1e-06)[None]).reshape(x.shape).astype(BF16)


def layer(x, w_up, w_down):
    lifted = jnp.dot(w_up, normalise(x), preferred_element_type=F32)
    bend = jnp.tanh(lifted * (GELU_A + GELU_B * (lifted * lifted)))
    twice_hidden = (lifted + lifted * bend).astype(BF16)
    return x + 0.5 * jnp.dot(w_down, twice_hidden, preferred_element_type=F32)


def kernel(
    prior,
    w_up,
    w_down,
    site,
    count,
    value,
    weight,
    out,
    fields,
    msg,
    state,
    mixed,
    flipped,
    rows_own,
    spread_w,
    up,
    down,
    code_own,
    code_out,
    code_in,
    smem_own,
    smem_in,
    obs_out,
    obs_in,
    load_sem,
    exchange_sem,
    near_send,
    near_recv,
    local_sem,
):
    me = lax.axis_index("member")
    left = lax.rem(me + PEERS - 1, PEERS)
    right = lax.rem(me + 1, PEERS)

    def tile_span(tile, j):
        return pl.ds(pl.multiple_of(tile * TILE + j * LANES, LANES), LANES)

    def load_pair(i, sem):
        for t in range(2):
            for j in range(BLOCKS):
                pltpu.make_async_copy(
                    prior.at[:, :, tile_span(peer_of(me, 2 * i + 1 + t), j)],
                    fields.at[i, t * BLOCKS + j, 0:CH],
                    load_sem.at[sem],
                ).start()

    def loaded(span, sem):
        block = fields.at[span, :, 0:CH]
        return pltpu.make_async_copy(block, block, load_sem.at[sem])

    load_pair(0, 0)

    def load_step(i, carry):
        load_pair(i, 1)
        return carry

    lax.fori_loop(1, PEERS // 2, load_step, 0)

    barrier = pltpu.get_barrier_semaphore()

    def greet(step, carry):
        pl.semaphore_signal(
            barrier, inc=1, device_id={"member": peer_of(me, step)}, device_id_type=MESH
        )
        return carry

    lax.fori_loop(1, PEERS, greet, 0)

    sites = site[...]
    channel = ((sites >> 7) * 6554) >> 15
    spot = sites - channel * STRIP

    def code(cell):
        row = ((cell >> 7) * HALVES + (channel >> 1)) * LANES + (cell & (LANES - 1))
        return 2 * row + (channel & 1)

    code_own[...] = code(jnp.clip(spot - HALO, 0, TILE - 1))
    code_out[0] = code(jnp.minimum(spot, HALO - 1) + (TILE - HALO))
    code_out[1] = code(jnp.maximum(spot - (HALO + TILE), 0))

    own_codes = pltpu.make_async_copy(code_own, smem_own, local_sem.at[0])
    own_codes.start()

    state[:, CH:FILL] = jnp.zeros((BLOCKS, FILL - CH, PEERS, 2, LANES), BF16)

    spread_w[...] = jnp.zeros_like(spread_w)
    for source, l in ((w_up, 0), (w_up, 1), (w_down, 0), (w_down, 1)):
        plain = source[:, l, :].astype(F32)
        for m in range(2):
            for b in range(HID // LANES):
                spread_w[m * 4 + b, pl.ds(m, CH, stride=2), :] = plain[:, b * LANES : (b + 1) * LANES]
        for b in range(2 * HID // LANES):
            span = slice(b * LANES, (b + 1) * LANES)
            if source is w_up:
                up[l, span, :] = spread_w[b].T.astype(BF16)
            else:
                down[l, :, span] = spread_w[b, 0:160].astype(BF16)

    def near_copy(src, dst, sem, target):
        return pltpu.make_async_remote_copy(
            src_ref=src,
            dst_ref=dst,
            send_sem=near_send.at[sem],
            recv_sem=near_recv.at[sem],
            device_id={"member": target},
            device_id_type=MESH,
        )

    code_left = near_copy(code_out.at[0], code_in.at[0], 0, left)
    code_right = near_copy(code_out.at[1], code_in.at[1], 1, right)
    def gather_copy(target, source):
        return pltpu.make_async_remote_copy(
            src_ref=msg.at[target, :, 0:CH],
            dst_ref=state.at[:, 0:CH, source],
            send_sem=exchange_sem.at[0],
            recv_sem=exchange_sem.at[1],
            device_id={"member": target},
            device_id_type=MESH,
        )

    def forecast(i, tiles):
        row = lax.broadcasted_iota(jnp.int32, (PAIR, LANES), 0)
        blocks = []
        for b in range(2 * BLOCKS):
            block = fields.at[i, b].reshape(2 * FILL, LANES)[0:PAIR, :].astype(F32)
            blocks.append(jnp.where(row < 2 * CH, block, 0.0))
        x = jnp.concatenate(blocks, axis=1)
        for l in range(2):
            x = layer(x, up[l, :, 0:PAIR], down[l, 0:PAIR])
        fill = jnp.zeros((2 * FILL - PAIR, LANES), F32)
        for t, tile in enumerate(tiles):
            for j in range(BLOCKS):
                b = t * BLOCKS + j
                block = jnp.concatenate([x[:, b * LANES : (b + 1) * LANES], fill], axis=0)
                msg.at[tile, j].reshape(2 * FILL, LANES)[...] = block.astype(BF16)

    def forecast_step(i, carry):
        tiles = (peer_of(me, 2 * i + 1), peer_of(me, 2 * i + 2))

        @pl.when(i == 0)
        def _():
            loaded(pl.ds(0, 1), 0).wait()

        @pl.when(i == 1)
        def _():
            loaded(pl.ds(1, PEERS // 2 - 1), 1).wait()

        forecast(i, tiles)

        @pl.when(i == 0)
        def _():
            pl.semaphore_wait(barrier, PEERS - 1)
            code_left.start()
            code_right.start()

        gather_copy(tiles[0], me).start()

        @pl.when(i < PEERS // 2 - 1)
        def _():
            gather_copy(tiles[1], me).start()

        return carry

    lax.fori_loop(0, PEERS // 2, forecast_step, 0)
    own_tile = pltpu.make_async_copy(msg.at[me, :, 0:CH], state.at[:, 0:CH, me], local_sem.at[1])
    own_tile.start()

    code_left.wait()
    code_right.wait()
    in_codes = pltpu.make_async_copy(code_in, smem_in, local_sem.at[2])
    in_codes.start()
    own_codes.wait()
    in_codes.wait()
    own_tile.wait()

    others = msg.at[0 : PEERS - 1, :, 0:CH]
    all_members = pltpu.make_async_remote_copy(
        src_ref=others,
        dst_ref=others,
        send_sem=exchange_sem.at[0],
        recv_sem=exchange_sem.at[1],
        device_id={"member": left},
        device_id_type=MESH,
    )
    all_members.wait_recv()

    row_id = lax.broadcasted_iota(jnp.int32, (LANES, LANES), 0)
    col_id = lax.broadcasted_iota(jnp.int32, (LANES, LANES), 1)
    unit = jnp.where(row_id == col_id, 1.0, 0.0).astype(BF16)

    def flip(rows):
        return lax.dot_general(
            unit, rows, (((1,), (1,)), ((), ())), preferred_element_type=F32
        )

    def flip_step(g, carry):
        for j in range(BLOCKS):
            slabs = state.at[j, pl.ds(g * GROUP, GROUP)].reshape(GROUP * MEMBERS, LANES)[...]
            turned = flip(slabs)
            for h in range(GROUP // 2):
                base = pl.multiple_of((j * HALVES + g * (GROUP // 2) + h) * LANES, LANES)
                flipped[pl.ds(base, LANES), :] = turned[:, h * LANES : (h + 1) * LANES]
        return carry

    lax.fori_loop(0, HALVES * 2 // GROUP, flip_step, 0)

    UNROLL = 16

    def gather(read_code, codes):
        def one(i, carry):
            for u in range(UNROLL):
                p = i * UNROLL + u
                rows_own[pl.ds(p, 1), :] = flipped[pl.ds(read_code(p) >> 1, 1), :]
            return carry

        lax.fori_loop(0, SLOTS // UNROLL, one, 0)
        both = flip(rows_own[...].astype(BF16))
        return jnp.where((codes & 1) == 0, both[:MEMBERS], both[MEMBERS:])

    obs_left = near_copy(obs_out.at[0], obs_in.at[0], 2, left)
    obs_right = near_copy(obs_out.at[1], obs_in.at[1], 3, right)
    obs_out[0] = gather(lambda p: smem_in[1, 0, p], code_in[1]).astype(BF16)
    obs_left.start()
    obs_out[1] = gather(lambda p: smem_in[0, 0, p], code_in[0]).astype(BF16)
    obs_right.start()
    obs_own = gather(lambda p: smem_own[0, p], code_own[...])
    obs_left.wait()
    obs_right.wait()

    below = spot < HALO
    above = spot >= HALO + TILE
    observed = jnp.where(
        below,
        obs_in[1].astype(F32),
        jnp.where(above, obs_in[0].astype(F32), obs_own),
    )
    slot_id = lax.broadcasted_iota(jnp.int32, (1, SLOTS), 1)
    live = slot_id < count[0]
    live = live & jnp.logical_not(below & (me == 0))
    live = live & jnp.logical_not(above & (me == PEERS - 1))
    rate = jnp.where(live, weight[...], 0.0)
    obs_mean = jnp.sum(observed, axis=0, keepdims=True) * (1.0 / MEMBERS)
    spread = observed - obs_mean
    departure = value[...] - obs_mean
    scaled = spread * rate
    right_side = jnp.concatenate(
        [spread, jnp.broadcast_to(departure, (MEMBERS, SLOTS))], axis=0
    )
    gram_drive = lax.dot_general(
        scaled,
        right_side,
        (((1,), (1,)), ((), ())),
        precision=lax.Precision.HIGHEST,
        preferred_element_type=F32,
    )
    row_id = lax.broadcasted_iota(jnp.int32, (MEMBERS, 2 * MEMBERS), 0)
    col_id = lax.broadcasted_iota(jnp.int32, (MEMBERS, 2 * MEMBERS), 1)
    swapped = pltpu.roll(gram_drive, MEMBERS, 1)
    system = jnp.where(
        col_id < MEMBERS,
        jnp.where(row_id == col_id, gram_drive + (MEMBERS - 1.0), gram_drive),
        gram_drive - 0.5 * swapped,
    )

    def eliminate(i, system):
        for j in range(0, 8, 2):
            row0, row1 = system[j : j + 1, :], system[j + 1 : j + 2, :]
            a, b = row0[:, j : j + 1], row0[:, j + 1 : j + 2]
            c, d = row1[:, j : j + 1], row1[:, j + 1 : j + 2]
            scale = 1.0 / (a * d - b * c)
            new0 = (row0 * d - row1 * b) * scale
            new1 = (row1 * a - row0 * c) * scale
            rest = system - system[:, j : j + 1] * new0 - system[:, j + 1 : j + 2] * new1
            system = jnp.where(row_id == j, new0, jnp.where(row_id == j + 1, new1, rest))
        system = jnp.concatenate([system[8:], system[:8]], axis=0)
        return pltpu.roll(system, LANES - 8, 1)

    system = lax.fori_loop(0, MEMBERS // 8, eliminate, system)
    mixing = system[:, :MEMBERS]
    mixing = mixing - jnp.sum(mixing, axis=0, keepdims=True) * (1.0 / MEMBERS)
    mixing_t = mixing.T
    coarse = mixing_t.astype(BF16)
    fine = (mixing_t - coarse.astype(F32)).astype(BF16)
    mixer = jnp.concatenate([coarse, fine], axis=1)

    def mix(j, channels):
        slabs = [state.at[j, c].reshape(MEMBERS, LANES)[...] for c in channels]
        slab = jnp.concatenate(slabs, axis=1)
        result = jnp.dot(
            mixer, jnp.concatenate([slab, slab], axis=0), preferred_element_type=F32
        ).astype(BF16)
        for k, c in enumerate(channels):
            mixed.at[j, c].reshape(MEMBERS, LANES)[...] = result[:, k * LANES : (k + 1) * LANES]

    def scatter_copy(j, target, tile):
        return pltpu.make_async_remote_copy(
            src_ref=mixed.at[j, 0:CH, target],
            dst_ref=out.at[:, :, tile_span(tile, j)],
            send_sem=exchange_sem.at[2],
            recv_sem=exchange_sem.at[3],
            device_id={"member": target},
            device_id_type=MESH,
        )

    def own_block(j):
        return pltpu.make_async_copy(
            mixed.at[j, 0:CH, me], out.at[:, :, tile_span(me, j)], local_sem.at[3 + j]
        )

    WIDE = 8
    for j in range(BLOCKS):

        def mix_step(i, carry):
            mix(j, [i * WIDE + k for k in range(WIDE)])
            return carry

        lax.fori_loop(0, FILL // WIDE, mix_step, 0)

        def send_step(i, carry):
            scatter_copy(j, peer_of(me, i), me).start()
            return carry

        lax.fori_loop(1, PEERS, send_step, 0)
        own_block(j).start()

    all_members.wait_send()
    for j in range(BLOCKS):
        own_block(j).wait()
    others = out.at[:, :, 0 : (PEERS - 1) * TILE]
    pltpu.make_async_remote_copy(
        src_ref=others,
        dst_ref=others,
        send_sem=exchange_sem.at[2],
        recv_sem=exchange_sem.at[3],
        device_id={"member": left},
        device_id_type=MESH,
    ).wait()


def copy_kernel(source, target, sem):
    copy = pltpu.make_async_copy(source, target, sem)
    copy.start()
    copy.wait()


def local(prior, w_up, w_down, site, count, value, weight):
    vmem = pl.BlockSpec(memory_space=pltpu.VMEM)
    smem = pl.BlockSpec(memory_space=pltpu.SMEM)
    anywhere = pl.BlockSpec(memory_space=pl.ANY)
    members, channels, cells = prior.shape
    result = pl.pallas_call(
        kernel,
        out_shape=jax.ShapeDtypeStruct((channels, members, cells), BF16),
        in_specs=[anywhere, vmem, vmem, vmem, smem, vmem, vmem],
        out_specs=anywhere,
        scratch_shapes=[
            pltpu.VMEM((PEERS // 2, 2 * BLOCKS, FILL, 2, LANES), BF16),
            pltpu.VMEM((PEERS, BLOCKS, FILL, 2, LANES), BF16),
            pltpu.VMEM((BLOCKS, FILL, PEERS, 2, LANES), BF16),
            pltpu.VMEM((BLOCKS, FILL, PEERS, 2, LANES), BF16),
            pltpu.VMEM((BLOCKS * HALVES * LANES, LANES), F32),
            pltpu.VMEM((SLOTS, LANES), F32),
            pltpu.VMEM((2 * HID // LANES, 2 * LANES, LANES), F32),
            pltpu.VMEM((2, 2 * HID, 2 * LANES), BF16),
            pltpu.VMEM((2, 160, 2 * HID), BF16),
            pltpu.VMEM((1, SLOTS), jnp.int32),
            pltpu.VMEM((2, 1, SLOTS), jnp.int32),
            pltpu.VMEM((2, 1, SLOTS), jnp.int32),
            pltpu.SMEM((1, SLOTS), jnp.int32),
            pltpu.SMEM((2, 1, SLOTS), jnp.int32),
            pltpu.VMEM((2, MEMBERS, SLOTS), BF16),
            pltpu.VMEM((2, MEMBERS, SLOTS), BF16),
            pltpu.SemaphoreType.DMA((2,)),
            pltpu.SemaphoreType.DMA((4,)),
            pltpu.SemaphoreType.DMA((4,)),
            pltpu.SemaphoreType.DMA((4,)),
            pltpu.SemaphoreType.DMA((3 + BLOCKS,)),
        ],
        compiler_params=pltpu.CompilerParams(
            collective_id=0, has_side_effects=True, vmem_limit_bytes=56 << 20
        ),
    )(
        prior.transpose(1, 0, 2),
        w_up.transpose(2, 0, 1),
        w_down.transpose(1, 0, 2),
        site,
        count,
        value,
        weight,
    )
    result = pl.pallas_call(
        copy_kernel,
        out_shape=jax.ShapeDtypeStruct(result.shape, BF16),
        in_specs=[vmem],
        out_specs=anywhere,
        scratch_shapes=[pltpu.SemaphoreType.DMA],
        compiler_params=pltpu.CompilerParams(vmem_limit_bytes=16 << 20),
    )(result)
    return result.transpose(1, 0, 2)


def solution(mesh):
    in_specs = (
        P("member", None, "space"),
        P(),
        P(),
        P(("member", "space"), None),
        P(("member", "space")),
        P(("member", "space"), None),
        P(("member", "space"), None),
    )
    return jax.shard_map(
        local,
        mesh=mesh,
        in_specs=in_specs,
        out_specs=P("member", None, "space"),
        check_vma=False,
    )
```

time: 189 us -> 125 us (0.66)
  Pallas kernels: 171 us -> 123 us
  local copies, waits for them, and re-layouts: 17 us -> 2.01 us
    pallas_call x1 -> x2, Pallas kernels: 171 us -> 123 us  [the longest x1 121 us: local(): pl.pallas_call(kernel, out_shape=jax.ShapeDtypeStruct((channels, members,...]
    pallas_call x1 -> x0, local copies, waits for them, and re-layouts: 7.69 us -> none  [local(): pl.pallas_call(kernel, out_shape=jax.ShapeDtypeStruct(prior.shape, BF16),...]
    unnamed x3 -> x2, local copies, waits for them, and re-layouts: 9.28 us -> 2.01 us
where the time goes in v2:
time: 125 us
  Pallas kernels  123 us (98%)
  local copies, waits for them, and re-layouts  2.01 us (2%)
    pallas_call x1, Pallas kernels, local(): pl.pallas_call(kernel, out_shape=jax.ShapeDtypeStruct((channels, members,...  121 us

profile of v2, /device:TPU:0, one launch (start us, length us, event | category | flops | bytes accessed | tf_op | source)
XLA Modules:
  0.0 125.2 jit_solution(11449710259896249217)
XLA Ops:
  0.7 120.7 %shard_map.73.source = bf16[73,2,12288]{2,1,0:T(2,128)(2,1)} custom-call(bf16[73,2,12288]{2,1,0:T(2,128)(2,1)} %bitcast.4, bf16[73,2,512]{2,1,0:T(2,128)(2,1)} %bitcast.5, bf16[73,2,512]{2,1,0:T(2,128)(2,1)} %bitcast.6, s32[1,512]{1,0:T(1,128)} %site.1, s32[1]{0:T(128)S(6)} %copy.8.count, f32[1,512]{1,0:T(1,128)} %value.1, f32[1,512]{1,0:T(1,128)} %weight.1), custom_call_target="tpu_custom_call" | custom-call | tf_op jit(solution)/shard_map/pallas_call | solution.py:415
  121.4 0.0 copy-start
  121.4 2.0 %copy-done = bf16[73,2,12288]{2,1,0:T(2,128)(2,1)S(1)} copy-done((bf16[73,2,12288]{2,1,0:T(2,128)(2,1)S(1)}, bf16[73,2,12288]{2,1,0:T(2,128)(2,1)}, u32[]{:S(2)}) %copy-start) | copy-done | bytes 3588120
  123.4 1.8 %shard_map.74 = bf16[73,2,12288]{2,1,0:T(2,128)(2,1)} custom-call(bf16[73,2,12288]{2,1,0:T(2,128)(2,1)S(1)} %copy-done), custom_call_target="tpu_custom_call" | custom-call | tf_op jit(solution)/shard_map/pallas_call | solution.py:455
Async XLA Ops:
  121.4 2.0 %copy-start = (bf16[73,2,12288]{2,1,0:T(2,128)(2,1)S(1)}, bf16[73,2,12288]{2,1,0:T(2,128)(2,1)}, u32[]{:S(2)}) copy-start(bf16[73,2,12288]{2,1,0:T(2,128)(2,1)} %shard_map.73.source) | copy-start | bytes 10764292

commit v3 on v2

--- a/solution.py
+++ b/solution.py
@@ -25,8 +25,9 @@
 LANES = 128
 BLOCKS = TILE // LANES
 ORDER = 25
+COPY_ROWS = 8
 GROUP = 4
-HALVES = 38
+HALVES = 40
 GELU_A = math.sqrt(2.0 / math.pi)
 GELU_B = GELU_A * 0.044715
 
@@ -108,17 +109,11 @@
                     load_sem.at[sem],
                 ).start()
 
-    def loaded(span, sem):
-        block = fields.at[span, :, 0:CH]
-        return pltpu.make_async_copy(block, block, load_sem.at[sem])
+    def loaded(i):
+        block = fields.at[i, :, 0:CH]
+        return pltpu.make_async_copy(block, block, load_sem.at[lax.rem(i, 2)])
 
     load_pair(0, 0)
-
-    def load_step(i, carry):
-        load_pair(i, 1)
-        return carry
-
-    lax.fori_loop(1, PEERS // 2, load_step, 0)
 
     barrier = pltpu.get_barrier_semaphore()
 
@@ -201,14 +196,11 @@
     def forecast_step(i, carry):
         tiles = (peer_of(me, 2 * i + 1), peer_of(me, 2 * i + 2))
 
-        @pl.when(i == 0)
+        @pl.when(i < PEERS // 2 - 1)
         def _():
-            loaded(pl.ds(0, 1), 0).wait()
-
-        @pl.when(i == 1)
-        def _():
-            loaded(pl.ds(1, PEERS // 2 - 1), 1).wait()
-
+            load_pair(i + 1, lax.rem(i + 1, 2))
+
+        loaded(i).wait()
         forecast(i, tiles)
 
         @pl.when(i == 0)
@@ -257,16 +249,16 @@
             unit, rows, (((1,), (1,)), ((), ())), preferred_element_type=F32
         )
 
-    def flip_step(g, carry):
-        for j in range(BLOCKS):
+    def flip_block(j):
+        def flip_step(g, carry):
             slabs = state.at[j, pl.ds(g * GROUP, GROUP)].reshape(GROUP * MEMBERS, LANES)[...]
             turned = flip(slabs)
             for h in range(GROUP // 2):
                 base = pl.multiple_of((j * HALVES + g * (GROUP // 2) + h) * LANES, LANES)
                 flipped[pl.ds(base, LANES), :] = turned[:, h * LANES : (h + 1) * LANES]
-        return carry
-
-    lax.fori_loop(0, HALVES * 2 // GROUP, flip_step, 0)
+            return carry
+
+        lax.fori_loop(0, HALVES * 2 // GROUP, flip_step, 0, unroll=4)
 
     UNROLL = 16
 
@@ -283,10 +275,14 @@
 
     obs_left = near_copy(obs_out.at[0], obs_in.at[0], 2, left)
     obs_right = near_copy(obs_out.at[1], obs_in.at[1], 3, right)
+    flip_block(0)
     obs_out[0] = gather(lambda p: smem_in[1, 0, p], code_in[1]).astype(BF16)
     obs_left.start()
+    flip_block(BLOCKS - 1)
     obs_out[1] = gather(lambda p: smem_in[0, 0, p], code_in[0]).astype(BF16)
     obs_right.start()
+    for j in range(1, BLOCKS - 1):
+        flip_block(j)
     obs_own = gather(lambda p: smem_own[0, p], code_own[...])
     obs_left.wait()
     obs_right.wait()
@@ -327,20 +323,27 @@
     )
 
     def eliminate(i, system):
+        sub = lax.broadcasted_iota(jnp.int32, (8, LANES), 0)
         for j in range(0, 8, 2):
-            row0, row1 = system[j : j + 1, :], system[j + 1 : j + 2, :]
-            a, b = row0[:, j : j + 1], row0[:, j + 1 : j + 2]
-            c, d = row1[:, j : j + 1], row1[:, j + 1 : j + 2]
+            row0 = jnp.broadcast_to(system[0, j : j + 1, :], (8, LANES))
+            row1 = jnp.broadcast_to(system[0, j + 1 : j + 2, :], (8, LANES))
+            a = jnp.broadcast_to(row0[:, j : j + 1], (8, LANES))
+            b = jnp.broadcast_to(row0[:, j + 1 : j + 2], (8, LANES))
+            c = jnp.broadcast_to(row1[:, j : j + 1], (8, LANES))
+            d = jnp.broadcast_to(row1[:, j + 1 : j + 2], (8, LANES))
             scale = 1.0 / (a * d - b * c)
             new0 = (row0 * d - row1 * b) * scale
             new1 = (row1 * a - row0 * c) * scale
-            rest = system - system[:, j : j + 1] * new0 - system[:, j + 1 : j + 2] * new1
-            system = jnp.where(row_id == j, new0, jnp.where(row_id == j + 1, new1, rest))
-        system = jnp.concatenate([system[8:], system[:8]], axis=0)
-        return pltpu.roll(system, LANES - 8, 1)
-
-    system = lax.fori_loop(0, MEMBERS // 8, eliminate, system)
-    mixing = system[:, :MEMBERS]
+            rest = system - system[:, :, j : j + 1] * new0 - system[:, :, j + 1 : j + 2] * new1
+            first = jnp.where(sub == j, new0, jnp.where(sub == j + 1, new1, rest[0]))
+            system = jnp.concatenate([first[None], rest[1:]], axis=0)
+        system = jnp.concatenate([system[1:], system[:1]], axis=0)
+        return pltpu.roll(system, LANES - 8, 2)
+
+    system = lax.fori_loop(
+        0, MEMBERS // 8, eliminate, system.reshape(MEMBERS // 8, 8, LANES)
+    )
+    mixing = system.reshape(MEMBERS, LANES)[:, :MEMBERS]
     mixing = mixing - jnp.sum(mixing, axis=0, keepdims=True) * (1.0 / MEMBERS)
     mixing_t = mixing.T
     coarse = mixing_t.astype(BF16)
@@ -401,10 +404,23 @@
     ).wait()
 
 
-def copy_kernel(source, target, sem):
-    copy = pltpu.make_async_copy(source, target, sem)
-    copy.start()
-    copy.wait()
+def copy_kernel(source, target, held, sem):
+    spans = [pl.ds(c, min(COPY_ROWS, CH - c)) for c in range(0, CH, COPY_ROWS)]
+    arrive = [
+        pltpu.make_async_copy(source.at[span], held.at[span], sem.at[0, k])
+        for k, span in enumerate(spans)
+    ]
+    leave = [
+        pltpu.make_async_copy(held.at[span], target.at[span], sem.at[1, k])
+        for k, span in enumerate(spans)
+    ]
+    for copy in arrive:
+        copy.start()
+    for k, copy in enumerate(leave):
+        arrive[k].wait()
+        copy.start()
+    for copy in leave:
+        copy.wait()
 
 
 def local(prior, w_up, w_down, site, count, value, weight):
@@ -455,10 +471,10 @@
     result = pl.pallas_call(
         copy_kernel,
         out_shape=jax.ShapeDtypeStruct(result.shape, BF16),
-        in_specs=[vmem],
+        in_specs=[anywhere],
         out_specs=anywhere,
-        scratch_shapes=[pltpu.SemaphoreType.DMA],
-        compiler_params=pltpu.CompilerParams(vmem_limit_bytes=16 << 20),
+        scratch_shapes=[pltpu.VMEM(result.shape, BF16), pltpu.SemaphoreType.DMA((2, 10))],
+        compiler_params=pltpu.CompilerParams(vmem_limit_bytes=56 << 20),
     )(result)
     return result.transpose(1, 0, 2)
 

time: 125 us -> 119 us (0.952)
  Pallas kernels: 123 us -> 118 us
  local copies, waits for them, and re-layouts: 2.01 us -> 0 us
    pallas_call x1, Pallas kernels: 121 us -> 115 us  [local(): pl.pallas_call(kernel, out_shape=jax.ShapeDtypeStruct((channels, members,...]
    unnamed x2 -> x0, local copies, waits for them, and re-layouts: 2.01 us -> none
where the time goes in v3:
time: 119 us; the launch traced here: 118 us
  Pallas kernels  118 us (99%)
    pallas_call x1, Pallas kernels, local(): pl.pallas_call(kernel, out_shape=jax.ShapeDtypeStruct((channels, members,...  115 us
    pallas_call x1, Pallas kernels, local(): pl.pallas_call(copy_kernel, out_shape=jax.ShapeDtypeStruct(result.shape,...  2.99 us

profile of v3, /device:TPU:0, one launch (start us, length us, event | category | flops | bytes accessed | tf_op | source)
XLA Modules:
  0.0 118.4 jit_solution(9738881565663383419)
XLA Ops:
  0.7 114.8 %shard_map.73.source = bf16[73,2,12288]{2,1,0:T(2,128)(2,1)} custom-call(bf16[73,2,12288]{2,1,0:T(2,128)(2,1)} %bitcast.4, bf16[73,2,512]{2,1,0:T(2,128)(2,1)} %bitcast.5, bf16[73,2,512]{2,1,0:T(2,128)(2,1)} %bitcast.6, s32[1,512]{1,0:T(1,128)} %site.1, s32[1]{0:T(128)S(6)} %copy.8.count, f32[1,512]{1,0:T(1,128)} %value.1, f32[1,512]{1,0:T(1,128)} %weight.1), custom_call_target="tpu_custom_call" | custom-call | tf_op jit(solution)/shard_map/pallas_call | solution.py:431
  115.4 3.0 %shard_map.74 = bf16[73,2,12288]{2,1,0:T(2,128)(2,1)} custom-call(bf16[73,2,12288]{2,1,0:T(2,128)(2,1)} %shard_map.73.source), custom_call_target="tpu_custom_call" | custom-call | tf_op jit(solution)/shard_map/pallas_call | solution.py:471

commit v4 on v3

--- a/solution.py
+++ b/solution.py
@@ -25,7 +25,7 @@
 LANES = 128
 BLOCKS = TILE // LANES
 ORDER = 25
-COPY_ROWS = 8
+COPY_ROWS = 15
 GROUP = 4
 HALVES = 40
 GELU_A = math.sqrt(2.0 / math.pi)
@@ -64,13 +64,18 @@
 
 def kernel(
     prior,
+    w_up_far,
+    w_down_far,
+    site_far,
+    count,
+    value_far,
+    weight_far,
+    out,
     w_up,
     w_down,
     site,
-    count,
     value,
     weight,
-    out,
     fields,
     msg,
     state,
@@ -87,12 +92,27 @@
     smem_in,
     obs_out,
     obs_in,
+    fetch_sem,
     load_sem,
     exchange_sem,
     near_send,
     near_recv,
     local_sem,
 ):
+    fetches = [
+        pltpu.make_async_copy(far, near, fetch_sem.at[k])
+        for k, (far, near) in enumerate(
+            (
+                (site_far, site),
+                (w_up_far, w_up),
+                (w_down_far, w_down),
+                (value_far, value),
+                (weight_far, weight),
+            )
+        )
+    ]
+    for fetch in fetches:
+        fetch.start()
     me = lax.axis_index("member")
     left = lax.rem(me + PEERS - 1, PEERS)
     right = lax.rem(me + 1, PEERS)
@@ -125,6 +145,7 @@
 
     lax.fori_loop(1, PEERS, greet, 0)
 
+    fetches[0].wait()
     sites = site[...]
     channel = ((sites >> 7) * 6554) >> 15
     spot = sites - channel * STRIP
@@ -143,7 +164,9 @@
     state[:, CH:FILL] = jnp.zeros((BLOCKS, FILL - CH, PEERS, 2, LANES), BF16)
 
     spread_w[...] = jnp.zeros_like(spread_w)
-    for source, l in ((w_up, 0), (w_up, 1), (w_down, 0), (w_down, 1)):
+    for fetch in fetches[1:]:
+        fetch.wait()
+    for source, l in ((w_up, 0), (w_down, 0), (w_up, 1), (w_down, 1)):
         plain = source[:, l, :].astype(F32)
         for m in range(2):
             for b in range(HID // LANES):
@@ -252,13 +275,13 @@
     def flip_block(j):
         def flip_step(g, carry):
             slabs = state.at[j, pl.ds(g * GROUP, GROUP)].reshape(GROUP * MEMBERS, LANES)[...]
-            turned = flip(slabs)
             for h in range(GROUP // 2):
                 base = pl.multiple_of((j * HALVES + g * (GROUP // 2) + h) * LANES, LANES)
-                flipped[pl.ds(base, LANES), :] = turned[:, h * LANES : (h + 1) * LANES]
+                pair = slabs[h * LANES : (h + 1) * LANES]
+                flipped[pl.ds(base, LANES), :] = pair.T.astype(F32)
             return carry
 
-        lax.fori_loop(0, HALVES * 2 // GROUP, flip_step, 0, unroll=4)
+        lax.fori_loop(0, HALVES * 2 // GROUP, flip_step, 0, unroll=5)
 
     UNROLL = 16
 
@@ -324,18 +347,35 @@
 
     def eliminate(i, system):
         sub = lax.broadcasted_iota(jnp.int32, (8, LANES), 0)
-        for j in range(0, 8, 2):
-            row0 = jnp.broadcast_to(system[0, j : j + 1, :], (8, LANES))
-            row1 = jnp.broadcast_to(system[0, j + 1 : j + 2, :], (8, LANES))
-            a = jnp.broadcast_to(row0[:, j : j + 1], (8, LANES))
-            b = jnp.broadcast_to(row0[:, j + 1 : j + 2], (8, LANES))
-            c = jnp.broadcast_to(row1[:, j : j + 1], (8, LANES))
-            d = jnp.broadcast_to(row1[:, j + 1 : j + 2], (8, LANES))
+
+        def solve_pair(a, b, c, d):
             scale = 1.0 / (a * d - b * c)
-            new0 = (row0 * d - row1 * b) * scale
-            new1 = (row1 * a - row0 * c) * scale
-            rest = system - system[:, :, j : j + 1] * new0 - system[:, :, j + 1 : j + 2] * new1
-            first = jnp.where(sub == j, new0, jnp.where(sub == j + 1, new1, rest[0]))
+            return lambda p, q: ((p * d - q * b) * scale, (q * a - p * c) * scale)
+
+        for j in range(0, 8, 4):
+            rows = [jnp.broadcast_to(system[0, j + r : j + r + 1, :], (8, LANES)) for r in range(4)]
+            e = [[jnp.broadcast_to(r[:, j + k : j + k + 1], (8, LANES)) for k in range(4)] for r in rows]
+            upper = solve_pair(e[0][0], e[0][1], e[1][0], e[1][1])
+            new0, new1 = upper(rows[0], rows[1])
+            u02, u12 = upper(e[0][2], e[1][2])
+            u03, u13 = upper(e[0][3], e[1][3])
+            low2 = rows[2] - e[2][0] * new0 - e[2][1] * new1
+            low3 = rows[3] - e[3][0] * new0 - e[3][1] * new1
+            lower = solve_pair(
+                e[2][2] - e[2][0] * u02 - e[2][1] * u12,
+                e[2][3] - e[2][0] * u03 - e[2][1] * u13,
+                e[3][2] - e[3][0] * u02 - e[3][1] * u12,
+                e[3][3] - e[3][0] * u03 - e[3][1] * u13,
+            )
+            new2, new3 = lower(low2, low3)
+            new0 = new0 - u02 * new2 - u03 * new3
+            new1 = new1 - u12 * new2 - u13 * new3
+            rest = system
+            for k, new in enumerate((new0, new1, new2, new3)):
+                rest = rest - system[:, :, j + k : j + k + 1] * new
+            first = rest[0]
+            for k, new in enumerate((new0, new1, new2, new3)):
+                first = jnp.where(sub == j + k, new, first)
             system = jnp.concatenate([first[None], rest[1:]], axis=0)
         system = jnp.concatenate([system[1:], system[:1]], axis=0)
         return pltpu.roll(system, LANES - 8, 2)
@@ -359,10 +399,10 @@
         for k, c in enumerate(channels):
             mixed.at[j, c].reshape(MEMBERS, LANES)[...] = result[:, k * LANES : (k + 1) * LANES]
 
-    def scatter_copy(j, target, tile):
+    def scatter_copy(j, low, high, target, tile):
         return pltpu.make_async_remote_copy(
-            src_ref=mixed.at[j, 0:CH, target],
-            dst_ref=out.at[:, :, tile_span(tile, j)],
+            src_ref=mixed.at[j, low:high, target],
+            dst_ref=out.at[low:high, :, tile_span(tile, j)],
             send_sem=exchange_sem.at[2],
             recv_sem=exchange_sem.at[3],
             device_id={"member": target},
@@ -375,20 +415,21 @@
         )
 
     WIDE = 8
-    for j in range(BLOCKS):
+    for j, low, high in ((0, 0, 16), (0, 16, CH), (1, 0, CH), (2, 0, CH)):
 
         def mix_step(i, carry):
             mix(j, [i * WIDE + k for k in range(WIDE)])
             return carry
 
-        lax.fori_loop(0, FILL // WIDE, mix_step, 0)
+        lax.fori_loop(low // WIDE, -(-high // WIDE), mix_step, 0)
 
         def send_step(i, carry):
-            scatter_copy(j, peer_of(me, i), me).start()
+            scatter_copy(j, low, high, peer_of(me, i), me).start()
             return carry
 
         lax.fori_loop(1, PEERS, send_step, 0)
-        own_block(j).start()
+        if high == CH:
+            own_block(j).start()
 
     all_members.wait_send()
     for j in range(BLOCKS):
@@ -424,16 +465,20 @@
 
 
 def local(prior, w_up, w_down, site, count, value, weight):
-    vmem = pl.BlockSpec(memory_space=pltpu.VMEM)
     smem = pl.BlockSpec(memory_space=pltpu.SMEM)
     anywhere = pl.BlockSpec(memory_space=pl.ANY)
     members, channels, cells = prior.shape
     result = pl.pallas_call(
         kernel,
         out_shape=jax.ShapeDtypeStruct((channels, members, cells), BF16),
-        in_specs=[anywhere, vmem, vmem, vmem, smem, vmem, vmem],
+        in_specs=[anywhere] * 4 + [smem] + [anywhere] * 2,
         out_specs=anywhere,
         scratch_shapes=[
+            pltpu.VMEM((CH, 2, HID), BF16),
+            pltpu.VMEM((CH, 2, HID), BF16),
+            pltpu.VMEM((1, SLOTS), jnp.int32),
+            pltpu.VMEM((1, SLOTS), F32),
+            pltpu.VMEM((1, SLOTS), F32),
             pltpu.VMEM((PEERS // 2, 2 * BLOCKS, FILL, 2, LANES), BF16),
             pltpu.VMEM((PEERS, BLOCKS, FILL, 2, LANES), BF16),
             pltpu.VMEM((BLOCKS, FILL, PEERS, 2, LANES), BF16),
@@ -450,6 +495,7 @@
             pltpu.SMEM((2, 1, SLOTS), jnp.int32),
             pltpu.VMEM((2, MEMBERS, SLOTS), BF16),
             pltpu.VMEM((2, MEMBERS, SLOTS), BF16),
+            pltpu.SemaphoreType.DMA((5,)),
             pltpu.SemaphoreType.DMA((2,)),
             pltpu.SemaphoreType.DMA((4,)),
             pltpu.SemaphoreType.DMA((4,)),

time: 119 us -> 114 us (0.958)
  Pallas kernels: 118 us -> 114 us
    pallas_call x1, Pallas kernels: 115 us -> 111 us  [local(): pl.pallas_call(kernel, out_shape=jax.ShapeDtypeStruct((channels, members,...]
where the time goes in v4:
time: 114 us
  Pallas kernels  114 us (100%)
    pallas_call x1, Pallas kernels, local(): pl.pallas_call(kernel, out_shape=jax.ShapeDtypeStruct((channels, members,...  111 us
    pallas_call x1, Pallas kernels, local(): pl.pallas_call(copy_kernel, out_shape=jax.ShapeDtypeStruct(result.shape,...  3.09 us

profile of v4, /device:TPU:0, one launch (start us, length us, event | category | flops | bytes accessed | tf_op | source)
XLA Modules:
  0.0 114.3 jit_solution(6106190375742229509)
XLA Ops:
  0.7 110.6 %shard_map.73.source = bf16[73,2,12288]{2,1,0:T(2,128)(2,1)} custom-call(bf16[73,2,12288]{2,1,0:T(2,128)(2,1)} %bitcast.4, bf16[73,2,512]{2,1,0:T(2,128)(2,1)} %bitcast.5, bf16[73,2,512]{2,1,0:T(2,128)(2,1)} %bitcast.6, s32[1,512]{1,0:T(1,128)} %site_far.1, s32[1]{0:T(128)S(6)} %copy.8.count, f32[1,512]{1,0:T(1,128)} %value_far.1, f32[1,512]{1,0:T(1,128)} %weight_far.1), custom_call_target="tpu_custom_call" | custom-call | tf_op jit(solution)/shard_map/pallas_call | solution.py:471
  111.2 3.1 %shard_map.74 = bf16[73,2,12288]{2,1,0:T(2,128)(2,1)} custom-call(bf16[73,2,12288]{2,1,0:T(2,128)(2,1)} %shard_map.73.source), custom_call_target="tpu_custom_call" | custom-call | tf_op jit(solution)/shard_map/pallas_call | solution.py:517

commit v5 on v4

--- a/solution.py
+++ b/solution.py
@@ -24,7 +24,8 @@
 HID = 512
 LANES = 128
 BLOCKS = TILE // LANES
-ORDER = 25
+ORDER = 23
+OWN_STEP = 10
 COPY_ROWS = 15
 GROUP = 4
 HALVES = 40
@@ -38,6 +39,16 @@
     y = lax.rem(lax.rem(me // 4, 4) + lax.rem(off // 4, 4), 4)
     z = lax.rem(me // 16 + off // 16, 2)
     return z * 16 + y * 4 + x
+
+
+def pair_of(me, i):
+    turn = lax.rem(i + PEERS // 2 - OWN_STEP, PEERS // 2)
+    tiles = []
+    for t in range(2):
+        x = lax.rem(lax.rem(me, 4) + lax.rem(turn, 4) + 2 * t, 4)
+        y = lax.rem(lax.rem(me // 4, 4) + turn // 4 + 2 * t, 4)
+        tiles.append(lax.rem(me // 16 + t, 2) * 16 + y * 4 + x)
+    return tiles
 
 
 def normalise(x):
@@ -121,10 +132,10 @@
         return pl.ds(pl.multiple_of(tile * TILE + j * LANES, LANES), LANES)
 
     def load_pair(i, sem):
-        for t in range(2):
+        for t, tile in enumerate(pair_of(me, i)):
             for j in range(BLOCKS):
                 pltpu.make_async_copy(
-                    prior.at[:, :, tile_span(peer_of(me, 2 * i + 1 + t), j)],
+                    prior.at[:, :, tile_span(tile, j)],
                     fields.at[i, t * BLOCKS + j, 0:CH],
                     load_sem.at[sem],
                 ).start()
@@ -217,7 +228,7 @@
                 msg.at[tile, j].reshape(2 * FILL, LANES)[...] = block.astype(BF16)
 
     def forecast_step(i, carry):
-        tiles = (peer_of(me, 2 * i + 1), peer_of(me, 2 * i + 2))
+        tiles = pair_of(me, i)
 
         @pl.when(i < PEERS // 2 - 1)
         def _():
@@ -232,11 +243,11 @@
             code_left.start()
             code_right.start()
 
-        gather_copy(tiles[0], me).start()
-
-        @pl.when(i < PEERS // 2 - 1)
+        gather_copy(tiles[1], me).start()
+
+        @pl.when(i != OWN_STEP)
         def _():
-            gather_copy(tiles[1], me).start()
+            gather_copy(tiles[0], me).start()
 
         return carry
 
@@ -263,15 +274,6 @@
     )
     all_members.wait_recv()
 
-    row_id = lax.broadcasted_iota(jnp.int32, (LANES, LANES), 0)
-    col_id = lax.broadcasted_iota(jnp.int32, (LANES, LANES), 1)
-    unit = jnp.where(row_id == col_id, 1.0, 0.0).astype(BF16)
-
-    def flip(rows):
-        return lax.dot_general(
-            unit, rows, (((1,), (1,)), ((), ())), preferred_element_type=F32
-        )
-
     def flip_block(j):
         def flip_step(g, carry):
             slabs = state.at[j, pl.ds(g * GROUP, GROUP)].reshape(GROUP * MEMBERS, LANES)[...]
@@ -293,7 +295,13 @@
             return carry
 
         lax.fori_loop(0, SLOTS // UNROLL, one, 0)
-        both = flip(rows_own[...].astype(BF16))
+        both = jnp.concatenate(
+            [
+                rows_own[b * LANES : (b + 1) * LANES, :].astype(BF16).T
+                for b in range(SLOTS // LANES)
+            ],
+            axis=1,
+        ).astype(F32)
         return jnp.where((codes & 1) == 0, both[:MEMBERS], both[MEMBERS:])
 
     obs_left = near_copy(obs_out.at[0], obs_in.at[0], 2, left)

time: 114 us -> 113 us (level); the launches traced: 114 us -> 111 us
  Pallas kernels: 114 us -> 111 us
    pallas_call x1, Pallas kernels: 111 us -> 108 us  [local(): pl.pallas_call(kernel, out_shape=jax.ShapeDtypeStruct((channels, members,...]
where the time goes in v5:
time: 113 us; the launch traced here: 111 us
  Pallas kernels  111 us (98%)
    pallas_call x1, Pallas kernels, local(): pl.pallas_call(kernel, out_shape=jax.ShapeDtypeStruct((channels, members,...  108 us
    pallas_call x1, Pallas kernels, local(): pl.pallas_call(copy_kernel, out_shape=jax.ShapeDtypeStruct(result.shape,...  3.09 us

profile of v5, /device:TPU:0, one launch (start us, length us, event | category | flops | bytes accessed | tf_op | source)
XLA Modules:
  0.0 111.5 jit_solution(3031216778924089357)
XLA Ops:
  0.7 107.7 %shard_map.73.source = bf16[73,2,12288]{2,1,0:T(2,128)(2,1)} custom-call(bf16[73,2,12288]{2,1,0:T(2,128)(2,1)} %bitcast.4, bf16[73,2,512]{2,1,0:T(2,128)(2,1)} %bitcast.5, bf16[73,2,512]{2,1,0:T(2,128)(2,1)} %bitcast.6, s32[1,512]{1,0:T(1,128)} %site_far.1, s32[1]{0:T(128)S(6)} %copy.8.count, f32[1,512]{1,0:T(1,128)} %value_far.1, f32[1,512]{1,0:T(1,128)} %weight_far.1), custom_call_target="tpu_custom_call" | custom-call | tf_op jit(solution)/shard_map/pallas_call | solution.py:479
  108.4 3.1 %shard_map.74 = bf16[73,2,12288]{2,1,0:T(2,128)(2,1)} custom-call(bf16[73,2,12288]{2,1,0:T(2,128)(2,1)} %shard_map.73.source), custom_call_target="tpu_custom_call" | custom-call | tf_op jit(solution)/shard_map/pallas_call | solution.py:525

commit v6 on v5

--- a/solution.py
+++ b/solution.py
@@ -285,7 +285,7 @@
 
         lax.fori_loop(0, HALVES * 2 // GROUP, flip_step, 0, unroll=5)
 
-    UNROLL = 16
+    UNROLL = 32
 
     def gather(read_code, codes):
         def one(i, carry):
@@ -429,13 +429,19 @@
             mix(j, [i * WIDE + k for k in range(WIDE)])
             return carry
 
-        lax.fori_loop(low // WIDE, -(-high // WIDE), mix_step, 0)
+        lax.fori_loop(low // WIDE, -(-high // WIDE), mix_step, 0, unroll=2)
 
         def send_step(i, carry):
-            scatter_copy(j, low, high, peer_of(me, i), me).start()
+            tiles = pair_of(me, i)
+            scatter_copy(j, low, high, tiles[1], me).start()
+
+            @pl.when(i != OWN_STEP)
+            def _():
+                scatter_copy(j, low, high, tiles[0], me).start()
+
             return carry
 
-        lax.fori_loop(1, PEERS, send_step, 0)
+        lax.fori_loop(0, PEERS // 2, send_step, 0)
         if high == CH:
             own_block(j).start()
 

time: 113 us -> 111 us (0.982); the launches traced: 111 us -> 111 us
  no operation moved by 1% of the time
where the time goes in v6:
time: 111 us
  Pallas kernels  110 us (99%)
    pallas_call x1, Pallas kernels, local(): pl.pallas_call(kernel, out_shape=jax.ShapeDtypeStruct((channels, members,...  107 us
    pallas_call x1, Pallas kernels, local(): pl.pallas_call(copy_kernel, out_shape=jax.ShapeDtypeStruct(result.shape,...  3.09 us

profile of v6, /device:TPU:0, one launch (start us, length us, event | category | flops | bytes accessed | tf_op | source)
XLA Modules:
  0.0 110.7 jit_solution(16115104810089724742)
XLA Ops:
  0.7 106.9 %shard_map.73.source = bf16[73,2,12288]{2,1,0:T(2,128)(2,1)} custom-call(bf16[73,2,12288]{2,1,0:T(2,128)(2,1)} %bitcast.4, bf16[73,2,512]{2,1,0:T(2,128)(2,1)} %bitcast.5, bf16[73,2,512]{2,1,0:T(2,128)(2,1)} %bitcast.6, s32[1,512]{1,0:T(1,128)} %site_far.1, s32[1]{0:T(128)S(6)} %copy.8.count, f32[1,512]{1,0:T(1,128)} %value_far.1, f32[1,512]{1,0:T(1,128)} %weight_far.1), custom_call_target="tpu_custom_call" | custom-call | tf_op jit(solution)/shard_map/pallas_call | solution.py:485
  107.6 3.1 %shard_map.74 = bf16[73,2,12288]{2,1,0:T(2,128)(2,1)} custom-call(bf16[73,2,12288]{2,1,0:T(2,128)(2,1)} %shard_map.73.source), custom_call_target="tpu_custom_call" | custom-call | tf_op jit(solution)/shard_map/pallas_call | solution.py:531
